TPU v7x, 32 devices: a whole 2x2x4 slice. The times are simulated.
32 devices in a mesh: dp: 8 (over y, x, core), mp: 4 (over z).
Axes of the slice: x: 2, y: 2, z: 4, core: 2. Of those that a mesh axis runs over, the one named last changes fastest.
Arguments:
- tokens: bfloat16 [28672, 768], P(('dp', 'mp')), may hold values from -6 to 6
- clip_lengths: int32 [32, 8], P('dp'), may hold values from 1 to 256, 896 in all within a row
- gain_attn: bfloat16 [768], replicated, may hold values from 0.099609375 to 1.8984375
- shift_attn: bfloat16 [768], replicated, may hold values from -3 to 3
- w_qkv: bfloat16 [3, 768, 768], P(None, None, 'mp'), may hold values from -0.21875 to 0.21875
- bias_qv: bfloat16 [2, 768], P(None, 'mp'), may hold values from -3 to 3
- w_out: bfloat16 [768, 768], P('mp'), may hold values from -0.875 to 0.875
- bias_out: bfloat16 [768], replicated, may hold values from -2 to 2
- gain_mlp: bfloat16 [768], replicated, may hold values from 0.099609375 to 1.8984375
- shift_mlp: bfloat16 [768], replicated, may hold values from -3 to 3
- w_up: bfloat16 [768, 3072], P(None, 'mp'), may hold values from -0.21875 to 0.21875
- bias_up: bfloat16 [3072], P('mp'), may hold values from -3 to 3
- w_down: bfloat16 [3072, 768], P('mp'), may hold values from -0.109375 to 0.109375
- bias_down: bfloat16 [768], replicated, may hold values from -3 to 3
- cotangent: bfloat16 [28672, 768], P(('dp', 'mp')), may hold values from -6 to 6
Outputs:
- output: bfloat16 [28672, 768], P(('dp', 'mp'))
- grad_tokens: float32 [28672, 768], P(('dp', 'mp'))
- grad_gain_attn: float32 [768], P(('dp', 'mp'))
- grad_shift_attn: float32 [768], P(('dp', 'mp'))
- grad_w_qkv: float32 [3, 768, 768], P(None, 'dp', 'mp')
- grad_bias_qv: float32 [2, 768], P(None, ('mp', 'dp'))
- grad_w_out: float32 [768, 768], P('mp', 'dp')
- grad_bias_out: float32 [768], P(('dp', 'mp'))
- grad_gain_mlp: float32 [768], P(('dp', 'mp'))
- grad_shift_mlp: float32 [768], P(('dp', 'mp'))
- grad_w_up: float32 [768, 3072], P('dp', 'mp')
- grad_bias_up: float32 [3072], P(('mp', 'dp'))
- grad_w_down: float32 [3072, 768], P('mp', 'dp')
- grad_bias_down: float32 [768], P(('dp', 'mp'))
Inputs may be any that keep to these rules, and one draw needn't show every extreme that they name: `clip_lengths`: each row's 8 lengths sum to 896, and its longest is exactly 256; the row's last clip is padding.
All inputs are finite; a program needn't handle non-finite values.
Results may differ from a plain program's by a relative error of at most 0.025.
Values may be sent and summed in bfloat16 or wider, within the bound.
No kernel may reach another device: no remote copies, remote signals or barrier semaphores. Data moves between devices by JAX's collectives and lax.ppermute only.
A program may use at most 192 MiB of HBM per device.

v0:
```python
from functools import partial

import jax
import jax.numpy as jnp
from jax import lax
from jax.sharding import PartitionSpec as P

HEAD_DIM = 64


EPSILON = 1e-06
MASKED = -1e30


def normalize(values_in, gain_row, shift_row):
    centre = jnp.mean(values_in, axis=1, keepdims=True)
    centred = values_in - centre
    inverse = lax.rsqrt(jnp.mean(centred * centred, axis=1, keepdims=True) + EPSILON)
    unit_rows = centred * inverse
    return (unit_rows * gain_row + shift_row, unit_rows, inverse)


def normalize_back(upstream, unit_rows, inverse, gain_row):
    scaled = upstream * gain_row
    return inverse * (
        scaled
        - jnp.mean(scaled, axis=1, keepdims=True)
        - unit_rows * jnp.mean(scaled * unit_rows, axis=1, keepdims=True)
    )


def allowed_pairs(lengths, slot_count):
    clip_ends = jnp.cumsum(lengths)
    places = lax.broadcasted_iota(jnp.int32, (slot_count,), 0)
    segment = jnp.sum((clip_ends[None, :] <= places[:, None]).astype(jnp.int32), axis=1)
    padding = segment == lengths.shape[0] - 1
    same_clip = segment[:, None] == segment[None, :]
    return same_clip & (jnp.logical_not(padding)[None, :] | (places[:, None] == places[None, :]))


def row_scores(queries, keys_row, lengths, score_scale):
    allowed = allowed_pairs(lengths, queries.shape[0])
    scores = (
        jnp.einsum("ihd,jhd->hij", queries, keys_row, preferred_element_type=jnp.float32)
        * score_scale
    )
    return jnp.where(allowed[None], scores, MASKED)


def attend_forward(inputs, score_scale):
    queries, keys_row, values_row, lengths = inputs
    scores = row_scores(queries, keys_row, lengths, score_scale)
    highest = jnp.max(scores, axis=2, keepdims=True)
    exponent = jnp.exp(scores - highest)
    totals = jnp.sum(exponent, axis=2, keepdims=True)
    weights_low = (exponent / totals).astype(jnp.bfloat16)
    attended = jnp.einsum(
        "hij,jhd->ihd", weights_low, values_row, preferred_element_type=jnp.float32
    )
    return (attended.astype(jnp.bfloat16), highest[:, :, 0] + jnp.log(totals[:, :, 0]))


def attend_backward(inputs, score_scale):
    queries, keys_row, values_row, lengths, log_totals, upstream = inputs
    scores = row_scores(queries, keys_row, lengths, score_scale)
    weights = jnp.exp(scores - log_totals[:, :, None])
    grad_weights = jnp.einsum(
        "ihd,jhd->hij", upstream, values_row, preferred_element_type=jnp.float32
    )
    centre = jnp.sum(weights * grad_weights, axis=2, keepdims=True)
    grad_scores = (weights * (grad_weights - centre)).astype(jnp.bfloat16)
    grad_query = (
        jnp.einsum("hij,jhd->ihd", grad_scores, keys_row, preferred_element_type=jnp.float32)
        * score_scale
    )
    grad_key = (
        jnp.einsum("hij,ihd->jhd", grad_scores, queries, preferred_element_type=jnp.float32)
        * score_scale
    )
    grad_value = jnp.einsum(
        "hij,ihd->jhd", weights.astype(jnp.bfloat16), upstream, preferred_element_type=jnp.float32
    )
    return (
        grad_query.astype(jnp.bfloat16),
        grad_key.astype(jnp.bfloat16),
        grad_value.astype(jnp.bfloat16),
    )


def on_device(
    tokens,
    clip_lengths,
    gain_attn,
    shift_attn,
    w_qkv,
    bias_qv,
    w_out,
    bias_out,
    gain_mlp,
    shift_mlp,
    w_up,
    bias_up,
    w_down,
    bias_down,
    cotangent,
):
    gain_one = gain_attn.astype(jnp.float32)
    gain_two = gain_mlp.astype(jnp.float32)
    count_rows = clip_lengths.shape[0]
    local_width = w_qkv.shape[2]
    local_heads = local_width // HEAD_DIM
    score_scale = HEAD_DIM ** (-0.5)
    residual_in = tokens.astype(jnp.float32)
    normed_one, unit_one, inverse_one = normalize(
        residual_in, gain_one, shift_attn.astype(jnp.float32)
    )
    normed_one_low = normed_one.astype(jnp.bfloat16)
    gathered_one = lax.all_gather(normed_one_low, "mp", axis=0, tiled=True)
    all_tokens = gathered_one.shape[0]
    slot_count = all_tokens // count_rows
    head_shape = (count_rows, slot_count, local_heads, HEAD_DIM)
    projected = jnp.einsum("td,cde->cte", gathered_one, w_qkv, preferred_element_type=jnp.float32)
    bias_pair = bias_qv.astype(jnp.float32)
    queries = (projected[0] + bias_pair[0]).astype(jnp.bfloat16).reshape(head_shape)
    keys_all = projected[1].astype(jnp.bfloat16).reshape(head_shape)
    values_all = (projected[2] + bias_pair[1]).astype(jnp.bfloat16).reshape(head_shape)
    attended, log_totals = lax.map(
        partial(attend_forward, score_scale=score_scale),
        (queries, keys_all, values_all, clip_lengths),
    )
    attended_flat = attended.reshape(all_tokens, local_width)
    attn_sum = lax.psum_scatter(
        jnp.dot(attended_flat, w_out, preferred_element_type=jnp.float32).astype(jnp.bfloat16),
        "mp",
        scatter_dimension=0,
        tiled=True,
    ).astype(jnp.float32)
    residual_mid = residual_in + attn_sum + bias_out.astype(jnp.float32)
    normed_two, unit_two, inverse_two = normalize(
        residual_mid, gain_two, shift_mlp.astype(jnp.float32)
    )
    normed_two_low = normed_two.astype(jnp.bfloat16)
    gathered_two = lax.all_gather(normed_two_low, "mp", axis=0, tiled=True)
    hidden_pre = jnp.dot(gathered_two, w_up, preferred_element_type=jnp.float32) + bias_up.astype(
        jnp.float32
    )
    hidden_act, gelu_pull = jax.vjp(partial(jax.nn.gelu, approximate=False), hidden_pre)
    hidden_low = hidden_act.astype(jnp.bfloat16)
    mlp_sum = lax.psum_scatter(
        jnp.dot(hidden_low, w_down, preferred_element_type=jnp.float32).astype(jnp.bfloat16),
        "mp",
        scatter_dimension=0,
        tiled=True,
    ).astype(jnp.float32)
    result = (residual_mid + mlp_sum + bias_down.astype(jnp.float32)).astype(jnp.bfloat16)
    grad_rows = cotangent.astype(jnp.float32)
    grad_bias_down = jnp.sum(grad_rows, axis=0)
    grad_gathered = lax.all_gather(cotangent, "mp", axis=0, tiled=True)
    grad_w_down = jnp.einsum(
        "tf,td->fd", hidden_low, grad_gathered, preferred_element_type=jnp.float32
    )
    grad_act = jnp.einsum("td,fd->tf", grad_gathered, w_down, preferred_element_type=jnp.float32)
    grad_pre_low = gelu_pull(grad_act)[0].astype(jnp.bfloat16)
    grad_bias_up = jnp.sum(grad_pre_low.astype(jnp.float32), axis=0)
    grad_w_up = jnp.einsum(
        "td,tf->df", gathered_two, grad_pre_low, preferred_element_type=jnp.float32
    )
    grad_norm_two = lax.psum_scatter(
        jnp.einsum("tf,df->td", grad_pre_low, w_up, preferred_element_type=jnp.float32).astype(
            jnp.bfloat16
        ),
        "mp",
        scatter_dimension=0,
        tiled=True,
    ).astype(jnp.float32)
    grad_mixed = grad_rows + normalize_back(grad_norm_two, unit_two, inverse_two, gain_two)
    grad_gain_mlp = jnp.sum(grad_norm_two * unit_two, axis=0)
    grad_shift_mlp = jnp.sum(grad_norm_two, axis=0)
    grad_bias_out = jnp.sum(grad_mixed, axis=0)
    branch_grad = lax.all_gather(grad_mixed.astype(jnp.bfloat16), "mp", axis=0, tiled=True)
    grad_w_out = jnp.einsum(
        "te,td->ed", attended_flat, branch_grad, preferred_element_type=jnp.float32
    )
    grad_attended = jnp.einsum(
        "td,ed->te", branch_grad, w_out, preferred_element_type=jnp.float32
    ).astype(jnp.bfloat16)
    grad_query, grad_key, grad_value = lax.map(
        partial(attend_backward, score_scale=score_scale),
        (
            queries,
            keys_all,
            values_all,
            clip_lengths,
            log_totals,
            grad_attended.reshape(head_shape),
        ),
    )
    grad_heads = jnp.stack([grad_query, grad_key, grad_value]).reshape(3, all_tokens, local_width)
    grad_bias_qv = jnp.stack(
        [
            jnp.sum(grad_heads[0].astype(jnp.float32), axis=0),
            jnp.sum(grad_heads[2].astype(jnp.float32), axis=0),
        ]
    )
    grad_w_qkv = jnp.einsum(
        "td,cte->cde", gathered_one, grad_heads, preferred_element_type=jnp.float32
    )
    grad_norm_one = lax.psum_scatter(
        jnp.einsum("cte,cde->td", grad_heads, w_qkv, preferred_element_type=jnp.float32).astype(
            jnp.bfloat16
        ),
        "mp",
        scatter_dimension=0,
        tiled=True,
    ).astype(jnp.float32)
    grad_tokens = grad_mixed + normalize_back(grad_norm_one, unit_one, inverse_one, gain_one)
    grad_gain_attn = jnp.sum(grad_norm_one * unit_one, axis=0)
    grad_shift_attn = jnp.sum(grad_norm_one, axis=0)
    grad_w_qkv, grad_bias_qv, grad_w_out, grad_w_up, grad_bias_up, grad_w_down = (
        lax.psum_scatter(grad_w_qkv, "dp", scatter_dimension=1, tiled=True),
        lax.psum_scatter(grad_bias_qv, "dp", scatter_dimension=1, tiled=True),
        lax.psum_scatter(grad_w_out, "dp", scatter_dimension=1, tiled=True),
        lax.psum_scatter(grad_w_up, "dp", scatter_dimension=0, tiled=True),
        lax.psum_scatter(grad_bias_up, "dp", scatter_dimension=0, tiled=True),
        lax.psum_scatter(grad_w_down, "dp", scatter_dimension=1, tiled=True),
    )
    (
        grad_gain_attn,
        grad_shift_attn,
        grad_bias_out,
        grad_gain_mlp,
        grad_shift_mlp,
        grad_bias_down,
    ) = (
        lax.psum_scatter(grad_gain_attn, ("dp", "mp"), scatter_dimension=0, tiled=True),
        lax.psum_scatter(grad_shift_attn, ("dp", "mp"), scatter_dimension=0, tiled=True),
        lax.psum_scatter(grad_bias_out, ("dp", "mp"), scatter_dimension=0, tiled=True),
        lax.psum_scatter(grad_gain_mlp, ("dp", "mp"), scatter_dimension=0, tiled=True),
        lax.psum_scatter(grad_shift_mlp, ("dp", "mp"), scatter_dimension=0, tiled=True),
        lax.psum_scatter(grad_bias_down, ("dp", "mp"), scatter_dimension=0, tiled=True),
    )
    return (
        result,
        grad_tokens,
        grad_gain_attn,
        grad_shift_attn,
        grad_w_qkv,
        grad_bias_qv,
        grad_w_out,
        grad_bias_out,
        grad_gain_mlp,
        grad_shift_mlp,
        grad_w_up,
        grad_bias_up,
        grad_w_down,
        grad_bias_down,
    )


def solution(mesh):
    return jax.shard_map(
        on_device,
        mesh=mesh,
        in_specs=(
            P(("dp", "mp"), None),
            P("dp", None),
            P(),
            P(),
            P(None, None, "mp"),
            P(None, "mp"),
            P("mp", None),
            P(),
            P(),
            P(),
            P(None, "mp"),
            P("mp"),
            P("mp", None),
            P(),
            P(("dp", "mp"), None),
        ),
        out_specs=(
            P(("dp", "mp"), None),
            P(("dp", "mp"), None),
            P(("dp", "mp")),
            P(("dp", "mp")),
            P(None, "dp", "mp"),
            P(None, ("mp", "dp")),
            P("mp", "dp"),
            P(("dp", "mp")),
            P(("dp", "mp")),
            P(("dp", "mp")),
            P("dp", "mp"),
            P(("mp", "dp")),
            P("mp", "dp"),
            P(("dp", "mp")),
        ),
        check_vma=False,
    )
```

profile of v0, /device:TPU:8, one launch (start us, length us, event | category | flops | bytes accessed | tf_op | source)
XLA Modules:
  0.0 1294.7 jit_solution(2757836400235333816)
XLA Ops:
  14.8 100.6 %all-gather.5.cloned.1.call-done = bf16[3584,768]{1,0:T(8,128)(2,1)} async-done(((bf16[896,768]{1,0:T(8,128)(2,1)}), bf16[3584,768]{1,0:T(8,128)(2,1)}) %all-gather.5.cloned.1.call-update) | async-done | bytes 5505040 | tf_op jit(solution)/shard_map/all_gather | solution.py:118
  145.6 46.5 %while.26 = (s32[]{:T(128)}, bf16[4,896,3,64]{1,3,2,0:T(8,128)(2,1)}, f32[4,3,896]{2,1,0:T(4,128)S(1)}, bf16[4,896,3,64]{1,3,2,0:T(8,128)(2,1)}, s32[4,8]{1,0:T(...) while((s32[]{:T(128)}, ...), condition=%wide.region_7.8_spmd, body=%wide.region_2.7_spmd.sunk | while | flops 648867136 | bytes 33600528 | solution.py:127
  200.7 98.7 %reduce-scatter.14.cloned.1.call-done = bf16[896,768]{1,0:T(8,128)(2,1)} async-done(((bf16[3584,768]{1,0:T(8,128)(2,1)}), bf16[896,768]{1,0:T(8,128)(2,1)}) %reduce-scatter.14.cloned.1.call-update) | async-done | bytes 1376272 | tf_op jit(solution)/shard_map/reduce_scatter | solution.py:132
  304.7 99.5 %all-gather.7.cloned.1.call-done = bf16[3584,768]{1,0:T(8,128)(2,1)} async-done(((bf16[896,768]{1,0:T(8,128)(2,1)}), bf16[3584,768]{1,0:T(8,128)(2,1)}) %all-gather.7.cloned.1.call-update) | async-done | bytes 5505040 | tf_op jit(solution)/shard_map/all_gather | solution.py:143
  404.2 11.9 fusion.106
  416.1 90.2 %all-gather.9.cloned.1.call-done = bf16[3584,768]{1,0:T(8,128)(2,1)} async-done(((bf16[896,768]{1,0:T(8,128)(2,1)}), bf16[3584,768]{1,0:T(8,128)(2,1)}) %all-gather.9.cloned.1.call-update) | async-done | bytes 5505040 | tf_op jit(solution)/shard_map/all_gather | solution.py:158
  506.4 32.4 %convert_reduce_fusion.2 = (f32[768]{0:T(1024)}, bf16[3584,768]{1,0:T(8,128)(2,1)S(1)}, f32[3584,768]{1,0:T(8,128)}) fusion(f32[3584,768]{1,0:T(8,128)} %fusion.106, f32[768]{0:T(1024)S(1)} %convert_element_type.154, bf16[3584,768]{1,0:T(8,128)(2,1)} %all-gather.9.cloned.1.call-done, bf16[768,768]{1,0:T(8,128)(2,1)S(1)} %copy-done), kind=kOutput, calls=%fused_computation.81 | convolution fusion | flops 4434295808 | bytes 34215936 | tf_op jit(solution)/shard_map/td,fd->tf/dot_general | solution.py:162
  548.1 8.4 multiply_convert_fusion.1
  565.8 81.2 %reduce-scatter.18.cloned.1.call-done = bf16[896,768]{1,0:T(8,128)(2,1)} async-done(((bf16[3584,768]{1,0:T(8,128)(2,1)}), bf16[896,768]{1,0:T(8,128)(2,1)}) %reduce-scatter.18.cloned.1.call-update) | async-done | bytes 1376272 | tf_op jit(solution)/shard_map/reduce_scatter | solution.py:168
  651.0 96.8 %reduce-scatter.16.cloned.1.call-done = bf16[896,768]{1,0:T(8,128)(2,1)} async-done(((bf16[3584,768]{1,0:T(8,128)(2,1)}), bf16[896,768]{1,0:T(8,128)(2,1)}) %reduce-scatter.16.cloned.1.call-update) | async-done | bytes 1376272 | tf_op jit(solution)/shard_map/reduce_scatter | solution.py:149
  755.8 100.1 %all-gather.11.cloned.1.call-done = bf16[3584,768]{1,0:T(8,128)(2,1)} async-done(((bf16[896,768]{1,0:T(8,128)(2,1)}), bf16[3584,768]{1,0:T(8,128)(2,1)}) %all-gather.11.cloned.1.call-update) | async-done | bytes 5505040 | tf_op jit(solution)/shard_map/all_gather | solution.py:180
  868.5 134.7 %while.27 = (s32[]{:T(128)}, bf16[4,896,3,64]{1,3,2,0:T(8,128)(2,1)}, bf16[4,896,3,64]{1,3,2,0:T(8,128)(2,1)}, bf16[4,896,3,64]{1,3,2,0:T(8,128)(2,1)}, bf16[4,8...) while((s32[]{:T(128)}, ...), condition=%wide.region_19.20_spmd, body=%wide.region_15.19_spmd.sunk | while | flops 1581624576 | bytes 142313616 | solution.py:187
  876.4 7.1 multiply_reduce_fusion.3
  883.5 11.2 multiply_convert_fusion.3
  917.2 11.2 multiply_convert_fusion.3
  950.8 11.2 multiply_convert_fusion.3
  984.4 11.2 multiply_convert_fusion.3
  1043.4 9.0 bitcast_convert_fusion
  1052.5 10.1 fusion.108
  1062.7 10.6 fusion.107
  1078.7 14.5 %all-reduce.9 = (f32[2,192]{1,0:T(2,128)S(1)}, f32[768]{0:T(1024)S(1)}) all-reduce(f32[2,192]{1,0:T(2,128)S(1)} %pad_maximum_fusion, f32[768]{0:T(1024)S(1)} %copy-done.27), channel_id=9, replica_groups=mesh['dp'=8,'mp'=4] {'dp'}, use_global_device_ids=true, to_apply=%region_30.31.clone | all-reduce | flops 1152 | bytes 9216
  1097.9 95.8 %reduce-scatter.20.cloned.1.call-done = bf16[896,768]{1,0:T(8,128)(2,1)} async-done(((bf16[3584,768]{1,0:T(8,128)(2,1)}), bf16[896,768]{1,0:T(8,128)(2,1)}) %reduce-scatter.20.cloned.1.call-update) | async-done | bytes 1376272 | tf_op jit(solution)/shard_map/reduce_scatter | solution.py:208
  1196.5 40.2 %all-reduce.8 = (f32[768]{0:T(1024)S(1)}, f32[768]{0:T(1024)S(1)}, f32[768]{0:T(1024)S(1)}, f32[768]{0:T(1024)S(1)}, f32[768]{0:T(1024)S(1)}, /*index=5*/f32[768]{0:T(1024)S(1)}) all-reduce(f32[768]{0:T(1024)S(1)} %get-tuple-element.237, f32[768]{0:T(1024)S(1)} %get-tuple-element.242, ...), channel_id=6, replica_groups=mesh['dp'=8,'mp'=4] {'dp','mp'}, use_global_device_ids=true, to_apply=%region_24.25.clone | all-reduce | flops 4608 | bytes 36864
  1244.1 43.6 %reduce-scatter.22.cloned.1.call-done = f32[96,768]{1,0:T(8,128)} async-done(((f32[768,768]{1,0:T(8,128)}), f32[96,768]{1,0:T(8,128)}) %reduce-scatter.22.cloned.1.call-update) | async-done | bytes 294928 | tf_op jit(solution)/shard_map/reduce_scatter | solution.py:223
  (283 shorter events, 282.3 us)
Async XLA Ops:
  7.2 499.2 %copy-start = (bf16[768,768]{1,0:T(8,128)(2,1)S(1)}, bf16[768,768]{1,0:T(8,128)(2,1)}, u32[]{:S(2)}) copy-start(bf16[768,768]{1,0:T(8,128)(2,1)} %param.31) | copy-start | bytes 3538948
  7.2 108.2 %all-gather.5.cloned.1.call-start = ((), (), s32[]{:S(2)}) async-start(), calls=%async_computation.8 | async-start | bytes 6881280 | tf_op jit(solution)/shard_map/all_gather | solution.py:118
  14.6 284.8 %reduce-scatter.14.cloned.1.call-start = ((), (), s32[]{:S(2)}) async-start(), calls=%async_computation.9 | async-start | bytes 6881280 | tf_op jit(solution)/shard_map/reduce_scatter | solution.py:132
  200.0 204.2 %all-gather.7.cloned.1.call-start = ((), (), s32[]{:S(2)}) async-start(), calls=%async_computation.10 | async-start | bytes 6881280 | tf_op jit(solution)/shard_map/all_gather | solution.py:143
  304.0 202.4 %all-gather.9.cloned.1.call-start = ((), (), s32[]{:S(2)}) async-start(), calls=%async_computation.12 | async-start | bytes 6881280 | tf_op jit(solution)/shard_map/all_gather | solution.py:158
  304.6 342.4 %reduce-scatter.18.cloned.1.call-start = ((), (), s32[]{:S(2)}) async-start(), calls=%async_computation.13 | async-start | bytes 6881280 | tf_op jit(solution)/shard_map/reduce_scatter | solution.py:168
  506.4 34.9 %copy-start.34 = (bf16[768,768]{1,0:T(8,128)(2,1)S(1)}, bf16[768,768]{1,0:T(8,128)(2,1)}, u32[]{:S(2)}) copy-start(bf16[768,768]{1,0:T(8,128)(2,1)} %param.29) | copy-start | bytes 3538948
  547.6 200.1 %reduce-scatter.16.cloned.1.call-start = ((), (), s32[]{:S(2)}) async-start(), calls=%async_computation.11 | async-start | bytes 6881280 | tf_op jit(solution)/shard_map/reduce_scatter | solution.py:149
  565.2 290.7 %all-gather.11.cloned.1.call-start = ((), (), s32[]{:S(2)}) async-start(), calls=%async_computation.14 | async-start | bytes 6881280 | tf_op jit(solution)/shard_map/all_gather | solution.py:180
  755.7 338.7 %reduce-scatter.28.cloned.1.call-start = ((), (), s32[]{:S(2)}) async-start(), calls=%async_computation.19 | async-start | bytes 884736
  1013.3 82.8 %reduce-scatter.26.cloned.1.call-start = ((), (), s32[]{:S(2)}) async-start(), calls=%async_computation.18 | async-start | bytes 2211840
  1043.4 150.4 %reduce-scatter.20.cloned.1.call-start = ((), (), s32[]{:S(2)}) async-start(), calls=%async_computation.15 | async-start | bytes 6881280 | tf_op jit(solution)/shard_map/reduce_scatter | solution.py:208
  1052.4 191.7 %reduce-scatter.24.cloned.1.call-start = ((), (), s32[]{:S(2)}) async-start(), calls=%async_computation.17 | async-start | bytes 2654208 | tf_op jit(solution)/shard_map/reduce_scatter | solution.py:225
  1062.6 10.7 copy-start.37
  1062.6 225.1 %reduce-scatter.22.cloned.1.call-start = ((), (), s32[]{:S(2)}) async-start(), calls=%async_computation.16 | async-start | bytes 2654208 | tf_op jit(solution)/shard_map/reduce_scatter | solution.py:223
  1073.2 120.5 %copy-start.5 = (bf16[896,768]{1,0:T(8,128)(2,1)S(1)}, bf16[896,768]{1,0:T(8,128)(2,1)}, u32[]{:S(2)}) copy-start(bf16[896,768]{1,0:T(8,128)(2,1)} %param.19) | copy-start | bytes 4128772
  1073.2 120.5 %copy-start.18 = (f32[896]{0:T(1024)S(1)}, f32[896]{0:T(1024)}, u32[]{:S(2)}) copy-start(f32[896]{0:T(1024)} %copy-done.17) | copy-start | bytes 10756
  1073.2 120.5 %copy-start.20 = (f32[768]{0:T(1024)S(1)}, f32[768]{0:T(1024)}, u32[]{:S(2)}) copy-start(f32[768]{0:T(1024)} %copy-done.19) | copy-start | bytes 9220
  1073.2 120.5 %copy-start.22 = (f32[896]{0:T(1024)S(1)}, f32[896]{0:T(1024)}, u32[]{:S(2)}) copy-start(f32[896]{0:T(1024)} %copy-done.21) | copy-start | bytes 10756
  1075.3 121.2 %copy-start.23 = (f32[768]{0:T(1024)S(1)}, f32[768]{0:T(1024)}, u32[]{:S(2)}) copy-start(f32[768]{0:T(1024)} %get-tuple-element.290) | copy-start | bytes 9220
  1075.3 121.2 %copy-start.24 = (f32[768]{0:T(1024)S(1)}, f32[768]{0:T(1024)}, u32[]{:S(2)}) copy-start(f32[768]{0:T(1024)} %get-tuple-element.299) | copy-start | bytes 9220
  1075.3 121.2 %copy-start.25 = (f32[768]{0:T(1024)S(1)}, f32[768]{0:T(1024)}, u32[]{:S(2)}) copy-start(f32[768]{0:T(1024)} %get-tuple-element.235) | copy-start | bytes 9220
  1075.3 121.2 %copy-start.26 = (f32[768]{0:T(1024)S(1)}, f32[768]{0:T(1024)}, u32[]{:S(2)}) copy-start(f32[768]{0:T(1024)} %get-tuple-element.241) | copy-start | bytes 9220
  1240.2 47.5 %copy-start.1 = (bf16[768,768]{1,0:T(8,128)(2,1)S(1)}, bf16[768,768]{1,0:T(8,128)(2,1)}, u32[]{:S(2)}) copy-start(bf16[768,768]{1,0:T(8,128)(2,1)} %param.31) | copy-start | bytes 3538948
  (36 other events, 120.1 us)
Sparse Core Ops, SparseCore 0:
  14.7 100.6 all-gather.4
  200.1 99.2 reduce-scatter.13
  304.1 100.0 all-gather.6
  405.6 100.7 all-gather.8
  547.7 99.2 reduce-scatter.17
  649.2 98.5 reduce-scatter.15
  755.8 100.0 all-gather.10
  1013.4 36.1 reduce-scatter.27
  1053.0 40.3 reduce-scatter.25
  1095.7 98.0 reduce-scatter.19
  1198.1 43.1 reduce-scatter.23
  1245.0 42.6 reduce-scatter.21
where the time goes:
time: 1300 us; the launch traced here: 1290 us
  waiting for transfers between devices  807 us (62%)
  matrix products  228 us (18%)
  other arithmetic  110 us (8%)
  local copies, waits for them, and re-layouts  76.8 us (6%)
  blocking collectives  54.6 us (4%)
  between operations  16.2 us (1%)
    all_gather x1, waiting for transfers between devices, on_device(): gathered_one = lax.all_gather(normed_one_low, 'mp', axis=0, tiled=True)  101 us
    all_gather x1, waiting for transfers between devices, on_device(): lax.all_gather(grad_mixed.astype(jnp.bfloat16), 'mp', axis=0, tiled=True)  100 us
    all_gather x1, waiting for transfers between devices, on_device(): gathered_two = lax.all_gather(normed_two_low, 'mp', axis=0, tiled=True)  99.5 us
    reduce_scatter x1, waiting for transfers between devices, on_device(): lax.psum_scatter(jnp.dot(attended_flat, w_out, preferred_element_type=jnp...  98.7 us
    reduce_scatter x1, waiting for transfers between devices, on_device(): lax.psum_scatter(jnp.dot(hidden_low, w_down, preferred_element_type=jnp.f...  96.8 us
    reduce_scatter x1, waiting for transfers between devices, on_device(): lax.psum_scatter(jnp.einsum('cte,cde->td', grad_heads, w_qkv, preferred_e...  95.8 us
    all_gather x1, waiting for transfers between devices, on_device(): grad_gathered = lax.all_gather(cotangent, 'mp', axis=0, tiled=True)  90.2 us
    reduce_scatter x1, waiting for transfers between devices, on_device(): lax.psum_scatter(jnp.einsum('tf,df->td', grad_pre_low, w_up, preferred_el...  81.2 us
  transfers between devices with their start and end apart: 12, of which 9 were waited for; matrix products, arithmetic and copies ran while one was open for 8% of the time, Pallas kernels for 0%

commit v1 on v0

v1 whole, which is shorter than its diff:
```python
from functools import partial

import jax
import jax.numpy as jnp
import numpy as np
from jax import lax
from jax.experimental import pallas as pl
from jax.experimental.pallas import tpu as pltpu
from jax.sharding import PartitionSpec as P

F32, BF = jnp.float32, jnp.bfloat16
HEAD_DIM = 64
MOST = 256
EPSILON = 1e-06
MASKED = -1e30
LOG2E = 1.4426950408889634
ROOT_HALF = 0.7071067811865476
RSQRT_2PI = 0.3989422804014327
PARTS = 8
KEY_BLOCK = 128
HIDDEN_BLOCK = 768
VMEM, SMEM, ANY = pltpu.VMEM, pltpu.SMEM, pl.ANY
SDS = jax.ShapeDtypeStruct


def _dot(a, b, i, j):
    return lax.dot_general(a, b, (((i,), (j,)), ((), ())), preferred_element_type=F32)


def nn(a, b):
    return _dot(a, b, 1, 0)


def nt(a, b):
    return _dot(a, b, 1, 1)


def tn(a, b):
    return _dot(a, b, 0, 0)


def tt(a, b):
    return _dot(a, b, 0, 1)


def vm():
    return pl.BlockSpec(memory_space=VMEM)


def cost(us):
    return pl.CostEstimate(flops=int(us * 1.0e9), bytes_accessed=1 << 20, transcendentals=0)


def windows(slots, width=256):
    out = []
    for q0 in range(0, slots, width):
        qn = min(width, slots - q0)
        lo = max(0, (q0 - MOST + 1) // 128 * 128)
        hi = min(slots, -(-(q0 + qn + MOST - 1) // 128) * 128)
        out.append((q0, qn, lo, hi - lo))
    return out


def segments(info, clips, shape, axis):
    place = lax.broadcasted_iota(jnp.int32, shape, axis)
    seg = jnp.zeros(shape, jnp.int32)
    for c in range(clips):
        seg = seg + jnp.where(place >= info[c], 1, 0)
    return jnp.where(seg == clips - 1, place + clips, seg)


def fill_mask(bias_sc, segc, segr, q0, qn, k0, w):
    for b in range(0, w, KEY_BLOCK):
        same = segc[k0 + b : k0 + b + KEY_BLOCK, :] == segr[:, q0 : q0 + qn]
        bias_sc[b : b + KEY_BLOCK, :qn] = jnp.where(same, 0.0, MASKED)


def fold(x, f):
    return f(x.reshape(x.shape[0] // 8, 8, x.shape[1]), axis=0)


def attend(tl, heads, scale, qkvT, kn, segc, segr, oT, lse, bias_sc, s_sc, p_sc):
    e, hd = heads * HEAD_DIM, HEAD_DIM
    for q0, qn, k0, w in tl:
        fill_mask(bias_sc, segc, segr, q0, qn, k0, w)
        for h in range(heads):
            q = qkvT[h * hd : (h + 1) * hd, q0 : q0 + qn]
            m = None
            for b in range(0, w, KEY_BLOCK):
                s = nn(kn[h, k0 + b : k0 + b + KEY_BLOCK, :], q) * scale + bias_sc[b : b + KEY_BLOCK, :qn]
                s_sc[b : b + KEY_BLOCK, :qn] = s
                mb = fold(s, jnp.max)
                m = mb if m is None else jnp.maximum(m, mb)
            m = jnp.max(m, axis=0, keepdims=True)
            total = None
            for b in range(0, w, KEY_BLOCK):
                p = jnp.exp2(s_sc[b : b + KEY_BLOCK, :qn] - m)
                p_sc[b : b + KEY_BLOCK, :qn] = p.astype(BF)
                lb = fold(p, jnp.sum)
                total = lb if total is None else total + lb
            total = jnp.sum(total, axis=0, keepdims=True)
            o = nn(qkvT[2 * e + h * hd : 2 * e + (h + 1) * hd, k0 : k0 + w], p_sc[:w, :qn])
            oT[h * hd : (h + 1) * hd, q0 : q0 + qn] = (o * (1.0 / total)).astype(BF)
            lse[h : h + 1, q0 : q0 + qn] = m + jnp.log2(total)


def unit(x):
    y = x - jnp.mean(x, axis=1, keepdims=True)
    inverse = lax.rsqrt(jnp.mean(y * y, axis=1, keepdims=True) + EPSILON)
    return y * inverse, inverse


def unit_back(up, n, inverse, gain):
    g = up * gain
    return inverse * (g - jnp.mean(g, axis=1, keepdims=True) - n * jnp.mean(g * n, axis=1, keepdims=True))


def normal(u):
    x = jnp.clip(u * ROOT_HALF, -3.832506856900711, 3.832506856900711)
    z = x * x
    a = 0.00022905065861350646
    for c in (0.0034082910107109506, 0.050955695062380861, 0.18520832239976145, 1.128379143519084):
        a = a * z + c
    b = -1.1791602954361697e-7
    for c in (
        0.000023547966471313185,
        0.0010179625278914885,
        0.014070470171167667,
        0.11098505178285362,
        0.49746925110067538,
        1.0,
    ):
        b = b * z + c
    return 0.5 + 0.5 * (x * a / b), jnp.exp2(u * u * (-0.5 * LOG2E)) * RSQRT_2PI


def pieces_in(info, at, refs, target, sem):
    copies = []
    for i, ref in enumerate(refs):
        for dst, src in target(ref, info[at + i]):
            copies.append(pltpu.make_async_copy(src, dst, sem))
    for c in copies:
        c.start()
    return copies


def blocks_out(info, at, source, place, keep, send, sem):
    n = source.shape[0] // PARTS
    copies = []
    for j in range(PARTS):
        dst = keep if j < PARTS // 2 else send
        row = pl.multiple_of(info[at + j] * n, n)
        copies.append(
            pltpu.make_async_copy(source.at[pl.ds(row, n)], dst.at[j % (PARTS // 2), pl.ds(place, n)], sem)
        )
    for c in copies:
        c.start()
    return copies


def weights_kernel(info, w_qkv, w_out, w0, piece):
    e = w_out.shape[0]
    for c in range(3):
        w0[c * e : (c + 1) * e, :] = w_qkv[c].T
    w0[3 * e :, :] = w_out[...]
    n = w0.shape[0] // PARTS
    piece[...] = w0[pl.ds(pl.multiple_of(info[24] * n, n), n), :]


def project_attend(clips, tl, heads, scale, r, info, n1, w, b, qkvT, oT, lse, kn, bias_sc, s_sc, p_sc):
    e = heads * HEAD_DIM
    slots = n1.shape[0]
    segc = segments(info, clips, (slots, 1), 0)
    segr = segments(info, clips, (1, slots), 1)
    for c in (1, 0, 2):
        t = (nt(w[c * e : (c + 1) * e, :], n1[...]) + b[c * e : (c + 1) * e, r : r + 1]).astype(BF)
        qkvT[c * e : (c + 1) * e, :] = t
        if c == 1:
            for h in range(heads):
                kn[h] = t[h * HEAD_DIM : (h + 1) * HEAD_DIM, :].T
    attend(tl, heads, scale, qkvT, kn, segc, segr, oT, lse, bias_sc, s_sc, p_sc)


def first_kernel(clips, tl, heads, scale, info, x, gain, shift, w, b, n1, qkvT, oT, lse, *scratch):
    rows = 128
    for i in range(0, x.shape[0], rows):
        n, _ = unit(x[i : i + rows, :].astype(F32))
        n1[i : i + rows, :] = (n * gain[...] + shift[...]).astype(BF)
    project_attend(clips, tl, heads, scale, 0, info, n1, w, b, qkvT, oT, lse, *scratch)


def attn_kernel(clips, tl, heads, scale, r, info, n1, b, *refs):
    pieces, (w, qkvT, oT, lse), scratch, sem = refs[:PARTS], refs[PARTS : PARTS + 4], refs[PARTS + 4 : -1], refs[-1]
    n = w.shape[0] // PARTS

    def target(ref, slot):
        return [(w.at[pl.ds(pl.multiple_of(slot * n, n), n)], ref)]

    for c in pieces_in(info, 8, pieces, target, sem):
        c.wait()
    project_attend(clips, tl, heads, scale, r, info, n1, w, b, qkvT, oT, lse, *scratch)


def mlp_chunk(info, n2, cot, wup, wdn, bup, out_acc, g_acc, keep, send, gb, hid, gp, up_sc, dn_sc, sem, fresh):
    H = wup.shape[1]
    n = n2.shape[1] // PARTS
    cuts = [slice(h, h + HIDDEN_BLOCK) for h in range(0, H, HIDDEN_BLOCK)]
    for s in cuts:
        u = nn(n2[...], wup[:, s]) + bup[:, s]
        ga = nt(cot[...], wdn[s, :])
        dist, dens = normal(u)
        hid[:, s] = (u * dist).astype(BF)
        g = (ga * (dist + u * dens)).astype(BF)
        gp[:, s] = g
        gb[:, s] = jnp.sum(g.astype(F32), axis=0, keepdims=True)
    dn_sc[...] = tn(cot[...], hid[...]).astype(BF)
    copies = blocks_out(info, 16, dn_sc, n, keep, send, sem)
    up_sc[...] = tn(n2[...], gp[...]).astype(BF)
    copies += blocks_out(info, 16, up_sc, 0, keep, send, sem)
    o, g = nn(hid[...], wdn[...]), nt(gp[...], wup[...])
    if fresh:
        out_acc[...] = o
        g_acc[...] = g
    else:
        out_acc[...] += o
        g_acc[...] += g
    return copies


def mid_kernel(info, x, bias_out, gain, shift, cot, o0, o1, o2, o3, w0, w1, w2, w3, wup, wdn, bup, *refs):
    mixed, n2, out_acc, g_acc, keep, send, gb, hid, gp, up_sc, dn_sc, sem = refs
    at = 3 * o0.shape[0]
    mixed[...] = x[...].astype(F32) + bias_out[...] + tn(o0[...], w0[at:, :])
    for o, w in ((o1, w1), (o2, w2), (o3, w3)):
        mixed[...] += tn(o[...], w[at:, :])
    rows = 128
    for i in range(0, x.shape[0], rows):
        n, _ = unit(mixed[i : i + rows, :])
        n2[i : i + rows, :] = (n * gain[...] + shift[...]).astype(BF)
    for c in mlp_chunk(info, n2, cot, wup, wdn, bup, out_acc, g_acc, keep, send, gb, hid, gp, up_sc, dn_sc, sem, True):
        c.wait()


def mlp_kernel(last, info, n2, cot, bup, out_in, g_in, *refs):
    if last:
        mixed, bias_down, gain = refs[:3]
        refs = refs[3:]
    pieces, refs = refs[:PARTS], refs[PARTS:]
    if last:
        result, grad_mixed, branch, vecs = refs[:4]
        refs = refs[4:]
        keep, send, gb, hid, gp, up_sc, dn_sc, wup, wdn, sem_in, sem = refs
        out_acc, g_acc = out_in, g_in
    else:
        out_acc, g_acc, keep, send, gb, hid, gp, up_sc, dn_sc, wup, wdn, sem_in, sem = refs
    n = wup.shape[0] // PARTS

    def target(ref, slot):
        row = pl.ds(pl.multiple_of(slot * n, n), n)
        return [(wup.at[row], ref.at[pl.ds(0, n)]), (wdn.at[row], ref.at[pl.ds(n, n)])]

    for c in pieces_in(info, 8, pieces, target, sem_in):
        c.wait()
    if not last:
        out_acc[...] = out_in[...]
        g_acc[...] = g_in[...]
    copies = mlp_chunk(info, n2, cot, wup, wdn, bup, out_acc, g_acc, keep, send, gb, hid, gp, up_sc, dn_sc, sem, False)
    if last:
        rows = 128
        sums = [0.0] * 4
        for i in range(0, n2.shape[0], rows):
            k = slice(i, i + rows)
            up, mid, c = g_acc[k, :], mixed[k, :], cot[k, :].astype(F32)
            result[k, :] = (mid + out_acc[k, :] + bias_down[...]).astype(BF)
            m, inverse = unit(mid)
            gm = c + unit_back(up, m, inverse, gain[...])
            grad_mixed[k, :] = gm
            branch[k, :] = gm.astype(BF)
            for j, v in enumerate((gm, up * m, up, c)):
                sums[j] = sums[j] + fold(v, jnp.sum)
        for j in range(4):
            vecs[j : j + 1, :] = jnp.sum(sums[j], axis=0, keepdims=True)
    for c in copies:
        c.wait()


def back_kernel(clips, tl, heads, scale, part, info, qkvT, w, gb, oT, n1, lse, dT, keep, send, small, *scratch):
    kn, vn, ga, bias_sc, p_sc, t_sc, pb_sc, ds_sc, dk, dv, acc, sem = scratch
    e, hd = heads * HEAD_DIM, HEAD_DIM
    slots = n1.shape[0]
    segc = segments(info, clips, (slots, 1), 0)
    segr = segments(info, clips, (1, slots), 1)
    ga[...] = nt(w[3 * e : 4 * e, :], gb[...]).astype(BF)
    for h in range(heads):
        kn[h] = qkvT[e + h * hd : e + (h + 1) * hd, :].T
        vn[h] = qkvT[2 * e + h * hd : 2 * e + (h + 1) * hd, :].T
    dk[...] = jnp.zeros_like(dk)
    dv[...] = jnp.zeros_like(dv)
    for q0, qn, k0, wide in tl:
        fill_mask(bias_sc, segc, segr, q0, qn, k0, wide)
        for h in range(heads):
            hs = slice(h * hd, (h + 1) * hd)
            q, go = qkvT[hs, q0 : q0 + qn], ga[hs, q0 : q0 + qn]
            total = lse[h : h + 1, q0 : q0 + qn]
            centre = None
            for b in range(0, wide, KEY_BLOCK):
                k, v = slice(b, b + KEY_BLOCK), slice(k0 + b, k0 + b + KEY_BLOCK)
                p = jnp.exp2(nn(kn[h, v, :], q) * scale + bias_sc[k, :qn] - total)
                t = p * nn(vn[h, v, :], go)
                p_sc[k, :qn] = p
                t_sc[k, :qn] = t
                pb_sc[k, :qn] = p.astype(BF)
                cb = fold(t, jnp.sum)
                centre = cb if centre is None else centre + cb
            centre = jnp.sum(centre, axis=0, keepdims=True)
            for b in range(0, wide, KEY_BLOCK):
                k = slice(b, b + KEY_BLOCK)
                ds_sc[k, :qn] = (t_sc[k, :qn] - p_sc[k, :qn] * centre).astype(BF)
            ds = ds_sc[:wide, :qn]
            dT[hs, q0 : q0 + qn] = (nn(qkvT[e + h * hd : e + (h + 1) * hd, k0 : k0 + wide], ds) * part).astype(BF)
            dk[hs, k0 : k0 + wide] += nt(q, ds)
            dv[hs, k0 : k0 + wide] += nt(go, pb_sc[:wide, :qn])
    dT[e : 2 * e, :] = (dk[...] * part).astype(BF)
    dT[2 * e : 3 * e, :] = dv[...].astype(BF)
    small[0:e, :] = jnp.sum(dT[0:e, :].astype(F32), axis=1, keepdims=True)
    small[e : 2 * e, :] = jnp.sum(dT[2 * e : 3 * e, :].astype(F32), axis=1, keepdims=True)
    acc[:, 0 : 3 * e] = tt(n1[...], dT[...]).astype(BF)
    acc[:, 3 * e : 4 * e] = tt(gb[...], oT[...]).astype(BF)
    for c in blocks_out(info, 16, acc, 0, keep, send, sem):
        c.wait()


def last_kernel(x, gain, grad_mixed, d0, d1, d2, d3, w0, w1, w2, w3, grad_tokens, vecs, g_sc):
    at = d0.shape[0]
    g_sc[...] = tn(d0[...], w0[:at, :])
    for dr, w in ((d1, w1), (d2, w2), (d3, w3)):
        g_sc[...] += tn(dr[...], w[:at, :])
    rows = 128
    sums = [0.0] * 2
    for i in range(0, x.shape[0], rows):
        k = slice(i, i + rows)
        up = g_sc[k, :]
        m, inverse = unit(x[k, :].astype(F32))
        grad_tokens[k, :] = grad_mixed[k, :] + unit_back(up, m, inverse, gain[...])
        for j, v in enumerate((up * m, up)):
            sums[j] = sums[j] + fold(v, jnp.sum)
    for j in range(2):
        vecs[j : j + 1, :] = jnp.sum(sums[j], axis=0, keepdims=True)


def on_device(
    places,
    planes,
    tokens,
    clip_lengths,
    gain_attn,
    shift_attn,
    w_qkv,
    bias_qv,
    w_out,
    bias_out,
    gain_mlp,
    shift_mlp,
    w_up,
    bias_up,
    w_down,
    bias_down,
    cotangent,
):
    T, D = tokens.shape
    clips = clip_lengths.shape[1]
    e = w_out.shape[0]
    heads = e // HEAD_DIM
    H = w_up.shape[1]
    n = D // PARTS
    rest = places // PARTS
    d, z = lax.axis_index("dp"), lax.axis_index("mp")
    hi = d // rest
    row = lambda v: v.astype(F32).reshape(1, -1)
    limit = lambda mb: pltpu.CompilerParams(vmem_limit_bytes=mb << 20)

    core = hi % 2
    first, second = jnp.where(core == 0, 2, 4), jnp.where(core == 0, 4, 2)
    both = lambda a, f, s: [a, a ^ f, a ^ s, a ^ 6]
    gathered = both(hi, first, second) + both(hi ^ 1, second, first)
    order = lambda a, f, s: [a, a ^ s, a ^ f, a ^ 6]
    exchanged = order(hi, first, second) + order(hi ^ 1, second, first)
    ends = jnp.cumsum(lax.dynamic_index_in_dim(clip_lengths, z, 0, keepdims=False))
    ends = jnp.concatenate([ends, jnp.zeros((8 - clips,), jnp.int32)])
    info = jnp.concatenate([ends, jnp.stack(gathered + exchanged + [hi]).astype(jnp.int32)])

    def over_plane(v, flip):
        return lax.ppermute(v, "dp", [(a, (((a // rest) ^ flip((a // rest) % 2)) * rest + a % rest)) for a in range(places)])

    to_core = lambda v: over_plane(v, lambda c: 1)
    to_first = lambda v: over_plane(v, lambda c: 4 if c else 2)
    to_second = lambda v: over_plane(v, lambda c: 2 if c else 4)

    def from_plane(v, r):
        return lax.ppermute(v, "mp", [(a, (a - r) % planes) for a in range(planes)])

    def to_plane(v, r):
        return lax.ppermute(v, "mp", [(a, (a + r) % planes) for a in range(planes)])

    far = [1, 3, 2]

    def spread(b):
        s1 = to_first(b)
        mine = [b, s1, to_second(b), to_second(s1)]
        return mine + [to_core(v) for v in mine]

    w0, piece = pl.pallas_call(
        weights_kernel,
        out_shape=(SDS((4 * e, D), BF), SDS((n, D), BF)),
        in_specs=[pl.BlockSpec(memory_space=SMEM), vm(), vm()],
        compiler_params=limit(16),
        cost_estimate=cost(2),
        name="weights",
    )(info, w_qkv, w_out)
    small_in = jnp.concatenate([bias_qv.reshape(-1), bias_up])
    got = {0: small_in}
    heads_from, units_from = {}, {}
    for r in far:
        heads_from[r] = from_plane(piece, r)
    for r in far:
        got[r] = from_plane(small_in, r)
    heads_in = {r: spread(heads_from[r]) for r in far}
    unit_piece = jnp.concatenate(
        [lax.dynamic_slice_in_dim(w_up, hi * n, n, 0), lax.dynamic_slice_in_dim(w_down, hi * n, n, 0)]
    )
    for r in far:
        units_from[r] = from_plane(unit_piece, r)
    units_in = {r: spread(units_from[r]) for r in far}
    biases = jnp.stack([got[r] for r in range(planes)]).astype(F32)
    cols = jnp.concatenate([biases[:, :e], jnp.zeros((planes, e), F32), biases[:, e : 2 * e]], axis=1).T
    bups = [biases[r : r + 1, 2 * e :] for r in range(planes)]

    tl = windows(T)
    wm, qm = max(t[3] for t in tl), max(t[1] for t in tl)
    scale = HEAD_DIM**-0.5 * LOG2E
    smem = pl.BlockSpec(memory_space=SMEM)
    anywhere = pl.BlockSpec(memory_space=ANY)
    attn_out = (SDS((3 * e, T), BF), SDS((e, T), BF), SDS((8, T), F32))
    attn_sc = [VMEM((heads, T, HEAD_DIM), BF), VMEM((wm, qm), F32), VMEM((wm, qm), F32), VMEM((wm, qm), BF)]
    n1, q0, o0, l0 = pl.pallas_call(
        partial(first_kernel, clips, tl, heads, scale),
        out_shape=(SDS((T, D), BF),) + attn_out,
        in_specs=[smem] + [vm()] * 5,
        scratch_shapes=attn_sc,
        compiler_params=limit(24),
        cost_estimate=cost(8),
        name="first",
    )(info, tokens, row(gain_attn), row(shift_attn), w0, cols)
    ws, qs, os, ls = {0: w0}, {0: q0}, {0: o0}, {0: l0}
    for r in far:
        ws[r], qs[r], os[r], ls[r] = pl.pallas_call(
            partial(attn_kernel, clips, tl, heads, scale, r),
            out_shape=(SDS((4 * e, D), BF),) + attn_out,
            in_specs=[smem, vm(), vm()] + [anywhere] * PARTS,
            scratch_shapes=attn_sc + [pltpu.SemaphoreType.DMA],
            compiler_params=limit(24),
            cost_estimate=cost(6),
            name=f"attn{r}",
        )(info, n1, cols, *heads_in[r])

    mlp_sc = [VMEM((T, H), BF)] * 2 + [VMEM((D, H), BF)] * 2
    grads_out = (SDS((PARTS // 2, 2 * n, H), BF),) * 2
    acc_out = (SDS((T, D), F32),) * 2
    keeps, sends, gbs = {}, {}, {}
    mixed, n2, out_acc, g_acc, keeps[0], sends[0], gbs[0] = pl.pallas_call(
        mid_kernel,
        out_shape=(SDS((T, D), F32), SDS((T, D), BF)) + acc_out + grads_out + (SDS((1, H), F32),),
        in_specs=[smem] + [vm()] * 16,
        out_specs=(vm(), vm(), vm(), vm(), anywhere, anywhere, vm()),
        scratch_shapes=mlp_sc + [pltpu.SemaphoreType.DMA],
        compiler_params=limit(40),
        cost_estimate=cost(14),
        name="mid",
    )(
        info,
        tokens,
        row(bias_out),
        row(gain_mlp),
        row(shift_mlp),
        cotangent,
        *(os[r] for r in range(planes)),
        *(ws[r] for r in range(planes)),
        w_up,
        w_down,
        bups[0],
    )
    for r in far:
        last = r == far[-1]
        extra = (mixed, row(bias_down), row(gain_mlp)) if last else ()
        extra_out = (SDS((T, D), BF), SDS((T, D), F32), SDS((T, D), BF), SDS((4, D), F32)) if last else acc_out
        res = pl.pallas_call(
            partial(mlp_kernel, last),
            out_shape=extra_out + grads_out + (SDS((1, H), F32),),
            in_specs=[smem] + [vm()] * (5 + len(extra)) + [anywhere] * PARTS,
            out_specs=(vm(),) * len(extra_out) + (anywhere, anywhere, vm()),
            scratch_shapes=mlp_sc
            + [VMEM((D, H), BF), VMEM((H, D), BF), pltpu.SemaphoreType.DMA, pltpu.SemaphoreType.DMA],
            compiler_params=limit(40),
            cost_estimate=cost(14 if last else 10),
            name=f"mlp{r}",
        )(info, n2, cotangent, bups[r], out_acc, g_acc, *extra, *units_in[r])
        if last:
            result, grad_mixed, branch, vec_mlp = res[:4]
        else:
            out_acc, g_acc = res[:2]
        keeps[r], sends[r], gbs[r] = res[len(extra_out) :]

    f32 = lambda v: v.astype(F32)

    def reduce_plane(keep, send):
        k = f32(keep) + f32(to_core(send))
        k = k[:2] + f32(to_first(k[2:].astype(BF)))
        k = k[0] + f32(to_second(k[1].astype(BF)))
        if rest > 1:
            groups = [[a * rest + b for b in range(rest)] for a in range(PARTS)]
            k = k.reshape(-1, n, k.shape[-1])
            k = lax.psum_scatter(k, "dp", scatter_dimension=1, axis_index_groups=groups, tiled=True)
            k = k.reshape(-1, k.shape[-1])
        return k

    def reduce_planes(parts):
        total = parts[0]
        for r in range(1, planes):
            total = total + f32(to_plane(parts[r].astype(BF), r))
        return total

    unit_grads = {r: reduce_plane(keeps[r], sends[r]) for r in [0] + far}

    V = VMEM
    back_sc = (
        [V((heads, T, HEAD_DIM), BF)] * 2
        + [V((e, T), BF)]
        + [V((wm, qm), F32)] * 3
        + [V((wm, qm), BF)] * 2
        + [V((e, T), F32)] * 2
        + [V((D, 4 * e), BF), pltpu.SemaphoreType.DMA]
    )
    ds, head_grads, smalls = {}, {}, {}
    for r in far + [0]:
        ds[r], keep, send, smalls[r] = pl.pallas_call(
            partial(back_kernel, clips, tl, heads, scale, HEAD_DIM**-0.5),
            out_shape=(SDS((3 * e, T), BF),) + (SDS((PARTS // 2, n, 4 * e), BF),) * 2 + (SDS((2 * e, 1), F32),),
            in_specs=[smem] + [vm()] * 6,
            out_specs=(vm(), anywhere, anywhere, vm()),
            scratch_shapes=back_sc,
            compiler_params=limit(32),
            cost_estimate=cost(11),
            name=f"back{r}",
        )(info, qs[r], ws[r], branch, os[r], n1, ls[r])
        head_grads[r] = reduce_plane(keep, send)

    grad_tokens, vec_attn = pl.pallas_call(
        last_kernel,
        out_shape=(SDS((T, D), F32), SDS((2, D), F32)),
        in_specs=[vm()] * 11,
        out_specs=(vm(), vm()),
        scratch_shapes=[VMEM((T, D), F32)],
        compiler_params=limit(32),
        cost_estimate=cost(7),
        name="last",
    )(
        tokens,
        row(gain_attn),
        grad_mixed,
        *(ds[r] for r in range(planes)),
        *(ws[r] for r in range(planes)),
    )

    vecs = jnp.concatenate([vec_mlp, vec_attn]).reshape(1, -1)
    per = jnp.concatenate(
        [jnp.concatenate([gbs[r], smalls[r].reshape(1, -1)], axis=1) for r in range(planes)], axis=1
    )
    small = jnp.concatenate([per, vecs], axis=1)
    step = 1
    while step < places:
        small = small + lax.ppermute(small, "dp", [(a, a ^ step) for a in range(places)])
        step *= 2
    width = H + 2 * e
    vecs = small[:, planes * width :]
    per = [small[:, r * width : (r + 1) * width] for r in range(planes)]
    own = jnp.concatenate([per[0], vecs], axis=1)
    total = own
    for r in range(1, planes):
        total = total + to_plane(jnp.concatenate([per[r], vecs], axis=1), r)
    total = total[0]
    cut = lambda v, at, size: lax.dynamic_slice_in_dim(v, at, size, v.ndim - 1)
    grad_bias_up = cut(total[:H], d * (H // places), H // places)
    grad_bias_qv = cut(total[H:width].reshape(2, e), d * (e // places), e // places)
    piece_of = D // (places * planes)
    g_bo, g_gm, g_sm, g_bd, g_ga, g_sa = cut(total[width:].reshape(6, D), (d * planes + z) * piece_of, piece_of)

    units = reduce_planes(unit_grads)
    m = D // places
    grad_w_up, grad_w_down = units[:m], units[m:].T
    hd = reduce_planes(head_grads)
    grad_w_qkv = hd[:, : 3 * e].reshape(m, 3, e).transpose(1, 0, 2)
    grad_w_out = hd[:, 3 * e :].T
    return (
        result,
        grad_tokens,
        g_ga,
        g_sa,
        grad_w_qkv,
        grad_bias_qv,
        grad_w_out,
        g_bo,
        g_gm,
        g_sm,
        grad_w_up,
        grad_bias_up,
        grad_w_down,
        g_bd,
    )


def solution(mesh):
    return jax.shard_map(
        partial(on_device, mesh.shape["dp"], mesh.shape["mp"]),
        mesh=mesh,
        in_specs=(
            P(("dp", "mp"), None),
            P("dp", None),
            P(),
            P(),
            P(None, None, "mp"),
            P(None, "mp"),
            P("mp", None),
            P(),
            P(),
            P(),
            P(None, "mp"),
            P("mp"),
            P("mp", None),
            P(),
            P(("dp", "mp"), None),
        ),
        out_specs=(
            P(("dp", "mp"), None),
            P(("dp", "mp"), None),
            P(("dp", "mp")),
            P(("dp", "mp")),
            P(None, "dp", "mp"),
            P(None, ("mp", "dp")),
            P("mp", "dp"),
            P(("dp", "mp")),
            P(("dp", "mp")),
            P(("dp", "mp")),
            P("dp", "mp"),
            P(("mp", "dp")),
            P("mp", "dp"),
            P(("dp", "mp")),
        ),
        check_vma=False,
    )
```

time: 1300 us -> 424 us (0.33)
  waiting for transfers between devices: 807 us -> 94.8 us
  matrix products: 228 us -> 0 us
  Pallas kernels: 0 us -> 174 us
  other arithmetic: 110 us -> 20.6 us
  starting transfers between devices: 1.11 us -> 67.7 us
  blocking collectives: 54.6 us -> 0 us
  local copies, waits for them, and re-layouts: 76.8 us -> 57.1 us
  between operations: 16.2 us -> 2.12 us
    reduce_scatter x6 -> x0, waiting for transfers between devices: 416 us -> none  [the longest x1 98.7 us: on_device(): lax.psum_scatter(jnp.dot(attended_flat, w_out, preferred_element_type=jnp...]
    all_gather x4 -> x0, waiting for transfers between devices: 390 us -> none  [the longest x1 101 us: on_device(): gathered_one = lax.all_gather(normed_one_low, 'mp', axis=0, tiled=True)]
    dot_general x38 -> x0, matrix products: 216 us -> none  [the longest x1 32.4 us: on_device(): jnp.einsum('td,fd->tf', grad_gathered, w_down, preferred_element_type=jnp...]
    pallas_call x0 -> x14, Pallas kernels: none -> 174 us  [the longest x3 64.7 us: on_device(): pl.pallas_call(partial(mlp_kernel, last), out_shape=extra_out + grads_out...]
    ppermute x0 -> x87, waiting for transfers between devices: none -> 94.8 us  [the longest x66 62.6 us: over_plane(): lax.ppermute(v, 'dp', [(a, (a // rest ^ flip(a // rest % 2)) * rest + a %...]
    ppermute x0 -> x87, starting transfers between devices: none -> 67.7 us  [the longest x66 38.7 us: over_plane(): lax.ppermute(v, 'dp', [(a, (a // rest ^ flip(a // rest % 2)) * rest + a %...]
    convert_element_type x17 -> x7, other arithmetic: 64.4 us -> 2.43 us  [the longest x6 2.4 us: reduce_planes(): total = total + f32(to_plane(parts[r].astype(BF), r))]
    unnamed x2 -> x0, blocking collectives: 54.6 us -> none
  transfers between devices with their start and end apart: 12 -> 87, of which waited for: 9 -> 27; matrix products, arithmetic and copies ran while one was open for 8% -> 6% of each run, Pallas kernels for 0% -> 23%
where the time goes in v1:
time: 424 us; the launch traced here: 416 us
  Pallas kernels  174 us (41%)
  waiting for transfers between devices  94.8 us (22%)
  starting transfers between devices  67.7 us (16%)
  local copies, waits for them, and re-layouts  57.1 us (13%)
  other arithmetic  20.6 us (5%)
    pallas_call x3, Pallas kernels, on_device(): pl.pallas_call(partial(mlp_kernel, last), out_shape=extra_out + grads_out...  64.7 us
    ppermute x66, waiting for transfers between devices, over_plane(): lax.ppermute(v, 'dp', [(a, (a // rest ^ flip(a // rest % 2)) * rest + a %...  62.6 us
    pallas_call x4, Pallas kernels, on_device(): pl.pallas_call(partial(back_kernel, clips, tl, heads, scale, HEAD_DIM **...  47.7 us
    unnamed x197, local copies, waits for them, and re-layouts  42.8 us
    ppermute x66, starting transfers between devices, over_plane(): lax.ppermute(v, 'dp', [(a, (a // rest ^ flip(a // rest % 2)) * rest + a %...  38.7 us
    pallas_call x3, Pallas kernels, on_device(): pl.pallas_call(partial(attn_kernel, clips, tl, heads, scale, r), out_shap...  24.3 us
    pallas_call x1, Pallas kernels, on_device(): pl.pallas_call(mid_kernel, out_shape=(SDS((T, D), F32), SDS((T, D), BF))...  21.3 us
    ppermute x9, waiting for transfers between devices, to_plane(): return lax.ppermute(v, 'mp', [(a, (a + r) % planes) for a in range(planes)])  19.4 us
  transfers between devices with their start and end apart: 87, of which 27 were waited for; matrix products, arithmetic and copies ran while one was open for 6% of the time, Pallas kernels for 23%

profile of v1, /device:TPU:8, one launch (start us, length us, event | category | flops | bytes accessed | tf_op | source)
XLA Modules:
  0.0 416.1 jit_solution(10692058269774277099)
XLA Ops:
  21.9 4.1 collective-permute-done.19.refs_0_
  43.5 6.9 %first.1 = (bf16[896,768]{1,0:T(8,128)(2,1)S(1)}, bf16[576,896]{1,0:T(8,128)(2,1)S(1)}, bf16[192,896]{1,0:T(8,128)(2,1)S(1)}, f32[8,896]{1,0:T(8,128)S(1)}) custom-call(s32[25]{0:T(128)S(1)} %copy-done.24, bf16[896,768]{1,0:T(8,128)(2,1)S(1)} %copy-done.27, f32[1,768]{1,0:T(1,128)S(1)} %reshape.158.gain, f32[1,768]{1,0:T(1,128)S(1)} %reshape.160.shift, ...), custom_call_target="tpu_custom_call" | custom-call | flops 8000000000 | bytes 1048576 | tf_op jit(solution)/shard_map/first/pallas_call | solution.py:445
  57.4 8.4 %attn3.1 = (bf16[768,768]{1,0:T(8,128)(2,1)S(1)}, bf16[576,896]{1,0:T(8,128)(2,1)S(1)}, bf16[192,896]{1,0:T(8,128)(2,1)S(1)}, f32[8,896]{1,0:T(8,128)S(1)}) custom-call(s32[25]{0:T(128)S(1)} %copy-done.24, bf16[896,768]{1,0:T(8,128)(2,1)S(1)} %get-tuple-element.76.n1, f32[576,4]{1,0:T(8,128)S(1)} %copy.37.b, ...), custom_call_target="tpu_custom_call" | custom-call | flops 6000000000 | bytes 1048576 | tf_op jit(solution)/shard_map/attn3/pallas_call | solution.py:456
  69.8 7.8 %attn2.1 = (bf16[768,768]{1,0:T(8,128)(2,1)S(1)}, bf16[576,896]{1,0:T(8,128)(2,1)S(1)}, bf16[192,896]{1,0:T(8,128)(2,1)S(1)}, f32[8,896]{1,0:T(8,128)S(1)}) custom-call(s32[25]{0:T(128)S(1)} %copy-done.24, bf16[896,768]{1,0:T(8,128)(2,1)S(1)} %get-tuple-element.76.n1, f32[576,4]{1,0:T(8,128)S(1)} %copy.37.b, ...), custom_call_target="tpu_custom_call" | custom-call | flops 6000000000 | bytes 1048576 | tf_op jit(solution)/shard_map/attn2/pallas_call | solution.py:456
  80.8 8.1 %attn1.1 = (bf16[768,768]{1,0:T(8,128)(2,1)S(1)}, bf16[576,896]{1,0:T(8,128)(2,1)S(1)}, bf16[192,896]{1,0:T(8,128)(2,1)S(1)}, f32[8,896]{1,0:T(8,128)S(1)}) custom-call(s32[25]{0:T(128)S(1)} %copy-done.24, bf16[896,768]{1,0:T(8,128)(2,1)S(1)} %get-tuple-element.76.n1, f32[576,4]{1,0:T(8,128)S(1)} %copy.37.b, ...), custom_call_target="tpu_custom_call" | custom-call | flops 6000000000 | bytes 1048576 | tf_op jit(solution)/shard_map/attn1/pallas_call | solution.py:456
  92.9 21.3 %mid.1 = (f32[896,768]{1,0:T(8,128)}, bf16[896,768]{1,0:T(8,128)(2,1)S(1)}, f32[896,768]{1,0:T(8,128)}, f32[896,768]{1,0:T(8,128)}, bf16[4,192,768]{2,1,0:T(8,12...) custom-call(s32[25]{0:T(128)S(1)} %copy-done.24, bf16[896,768]{1,0:T(8,128)(2,1)S(1)} %copy-done.28, ...), custom_call_target="tpu_custom_call" | custom-call | flops 14000000000 | bytes 1048576 | tf_op jit(solution)/shard_map/mid/pallas_call | solution.py:470
  119.6 20.6 %mlp1.1 = (f32[896,768]{1,0:T(8,128)S(1)}, f32[896,768]{1,0:T(8,128)S(1)}, bf16[4,192,768]{2,1,0:T(8,128)(2,1)S(1)}, bf16[4,192,768]{2,1,0:T(8,128)(2,1)S(1)}, f32[1,768]{1,0:T(1,128)S(1)}) custom-call(s32[25]{0:T(128)S(1)} %copy-done.25, bf16[896,768]{1,0:T(8,128)(2,1)S(1)} %get-tuple-element.84.n2, bf16[896,768]{1,0:T(8,128)(2,1)S(1)} %copy-done.26, ...), custom_call_target="tpu_custom_call" | custom-call | flops 10000000000 | bytes 1048576 | tf_op jit(solution)/shard_map/mlp1/pallas_call | solution.py:496
  146.8 20.6 %mlp3.1 = (f32[896,768]{1,0:T(8,128)S(1)}, f32[896,768]{1,0:T(8,128)S(1)}, bf16[4,192,768]{2,1,0:T(8,128)(2,1)S(1)}, bf16[4,192,768]{2,1,0:T(8,128)(2,1)S(1)}, f32[1,768]{1,0:T(1,128)S(1)}) custom-call(s32[25]{0:T(128)S(1)} %copy-done.25, bf16[896,768]{1,0:T(8,128)(2,1)S(1)} %copy-done.65, bf16[896,768]{1,0:T(8,128)(2,1)S(1)} %copy-done.26, ...), custom_call_target="tpu_custom_call" | custom-call | flops 10000000000 | bytes 1048576 | tf_op jit(solution)/shard_map/mlp3/pallas_call | solution.py:496
  170.6 23.5 %mlp2.1 = (bf16[896,768]{1,0:T(8,128)(2,1)}, f32[896,768]{1,0:T(8,128)S(1)}, bf16[896,768]{1,0:T(8,128)(2,1)S(1)}, f32[4,768]{1,0:T(4,128)S(1)}, bf16[4,192,768]...) custom-call(s32[25]{0:T(128)S(1)} %copy-done.25, bf16[896,768]{1,0:T(8,128)(2,1)S(1)} %copy-done.66, ...), custom_call_target="tpu_custom_call" | custom-call | flops 14000000000 | bytes 1048576 | tf_op jit(solution)/shard_map/mlp2/pallas_call | solution.py:496
  196.9 11.9 %back1.1 = (bf16[576,896]{1,0:T(8,128)(2,1)S(1)}, bf16[4,96,768]{2,1,0:T(8,128)(2,1)S(1)}, bf16[4,96,768]{2,1,0:T(8,128)(2,1)S(1)}, f32[384,1]{1,0:T(8,128)S(1)}) custom-call(s32[25]{0:T(128)S(1)} %copy-done.25, bf16[576,896]{1,0:T(8,128)(2,1)S(1)} %copy-done.63, bf16[768,768]{1,0:T(8,128)(2,1)S(1)} %copy-done.54, ...), custom_call_target="tpu_custom_call" | custom-call | flops 11000000512 | bytes 1048576 | tf_op jit(solution)/shard_map/back1/pallas_call | solution.py:545
  211.1 11.9 %back2.1 = (bf16[576,896]{1,0:T(8,128)(2,1)S(1)}, bf16[4,96,768]{2,1,0:T(8,128)(2,1)S(1)}, bf16[4,96,768]{2,1,0:T(8,128)(2,1)S(1)}, f32[384,1]{1,0:T(8,128)S(1)}) custom-call(s32[25]{0:T(128)S(1)} %copy-done.25, bf16[576,896]{1,0:T(8,128)(2,1)S(1)} %get-tuple-element.101.qkvT, bf16[768,768]{1,0:T(8,128)(2,1)S(1)} %copy-done.52, ...), custom_call_target="tpu_custom_call" | custom-call | flops 11000000512 | bytes 1048576 | tf_op jit(solution)/shard_map/back2/pallas_call | solution.py:545
  225.4 12.1 %back3.1 = (bf16[576,896]{1,0:T(8,128)(2,1)S(1)}, bf16[4,96,768]{2,1,0:T(8,128)(2,1)S(1)}, bf16[4,96,768]{2,1,0:T(8,128)(2,1)S(1)}, f32[384,1]{1,0:T(8,128)S(1)}) custom-call(s32[25]{0:T(128)S(1)} %copy-done.25, bf16[576,896]{1,0:T(8,128)(2,1)S(1)} %copy-done.61, bf16[768,768]{1,0:T(8,128)(2,1)S(1)} %copy-done.50, ...), custom_call_target="tpu_custom_call" | custom-call | flops 11000000512 | bytes 1048576 | tf_op jit(solution)/shard_map/back3/pallas_call | solution.py:545
  239.9 11.8 %back0.1 = (bf16[576,896]{1,0:T(8,128)(2,1)S(1)}, bf16[4,96,768]{2,1,0:T(8,128)(2,1)S(1)}, bf16[4,96,768]{2,1,0:T(8,128)(2,1)S(1)}, f32[384,1]{1,0:T(8,128)S(1)}) custom-call(s32[25]{0:T(128)S(1)} %copy-done.25, bf16[576,896]{1,0:T(8,128)(2,1)S(1)} %copy-done.68, bf16[768,768]{1,0:T(8,128)(2,1)S(1)} %copy-done.46, ...), custom_call_target="tpu_custom_call" | custom-call | flops 11000000512 | bytes 1048576 | tf_op jit(solution)/shard_map/back0/pallas_call | solution.py:545
  254.1 7.4 %last.1 = (f32[896,768]{1,0:T(8,128)}, f32[2,768]{1,0:T(2,128)S(1)}) custom-call(bf16[896,768]{1,0:T(8,128)(2,1)S(1)} %copy-done.28, f32[1,768]{1,0:T(1,128)S(1)} %reshape.158.gain, f32[896,768]{1,0:T(8,128)S(1)} %copy-done.48, bf16[576,896]{1,0:T(8,128)(2,1)S(1)} %get-tuple-element.97.d0, bf16[576,896]{1,0:T(8,128)(2,1)S(1)} %get-tuple-element.100.d1, ...), custom_call_target="tpu_custom_call" | custom-call | flops 7000000000 | bytes 1048576 | tf_op jit(solution)/shard_map/last/pallas_call | solution.py:557
  286.6 3.4 collective-permute-start.54
  312.5 4.2 %collective-permute-done.61 = bf16[2,96,768]{2,1,0:T(8,128)(2,1)S(1)} collective-permute-done((bf16[2,96,768]{2,1,0:T(8,128)(2,1)S(1)}, bf16[2,96,768]{2,1,0:T(8,128)(2,1)S(1)}, u32[]{:S(2)}, u32[]{:S(2)}) %collective-permute-start.61) | collective-permute-done | bytes 294944 | tf_op jit(solution)/shard_map/ppermute | solution.py:393
  327.4 5.8 %collective-permute-done.62 = bf16[96,768]{1,0:T(8,128)(2,1)S(1)} collective-permute-done((bf16[96,768]{1,0:T(8,128)(2,1)S(1)}, bf16[96,768]{1,0:T(8,128)(2,1)S(1)}, u32[]{:S(2)}, u32[]{:S(2)}) %collective-permute-start.62) | collective-permute-done | bytes 147488 | tf_op jit(solution)/shard_map/ppermute | solution.py:393
  334.0 4.3 %collective-permute-done.66 = bf16[96,768]{1,0:T(8,128)(2,1)S(1)} collective-permute-done((bf16[96,768]{1,0:T(8,128)(2,1)S(1)}, bf16[96,768]{1,0:T(8,128)(2,1)S(1)}, u32[]{:S(2)}, u32[]{:S(2)}) %collective-permute-start.66) | collective-permute-done | bytes 147488 | tf_op jit(solution)/shard_map/ppermute | solution.py:393
  339.2 4.3 %collective-permute-done.70 = bf16[96,768]{1,0:T(8,128)(2,1)S(1)} collective-permute-done((bf16[96,768]{1,0:T(8,128)(2,1)S(1)}, bf16[96,768]{1,0:T(8,128)(2,1)S(1)}, u32[]{:S(2)}, u32[]{:S(2)}) %collective-permute-start.70) | collective-permute-done | bytes 147488 | tf_op jit(solution)/shard_map/ppermute | solution.py:393
  352.6 7.3 %collective-permute-done.76 = bf16[2,192,768]{2,1,0:T(8,128)(2,1)S(1)} collective-permute-done((bf16[2,192,768]{2,1,0:T(8,128)(2,1)S(1)}, bf16[2,192,768]{2,1,0:T(8,128)(2,1)S(1)}, u32[]{:S(2)}, u32[]{:S(2)}) %collective-permute-start.76) | collective-permute-done | bytes 589856 | tf_op jit(solution)/shard_map/ppermute | solution.py:393
  361.6 6.9 %collective-permute-done.80 = bf16[2,192,768]{2,1,0:T(8,128)(2,1)S(1)} collective-permute-done((bf16[2,192,768]{2,1,0:T(8,128)(2,1)S(1)}, bf16[2,192,768]{2,1,0:T(8,128)(2,1)S(1)}, u32[]{:S(2)}, u32[]{:S(2)}) %collective-permute-start.80) | collective-permute-done | bytes 589856 | tf_op jit(solution)/shard_map/ppermute | solution.py:393
  369.6 11.4 %collective-permute-done.84 = bf16[2,192,768]{2,1,0:T(8,128)(2,1)S(1)} collective-permute-done((bf16[2,192,768]{2,1,0:T(8,128)(2,1)S(1)}, bf16[2,192,768]{2,1,0:T(8,128)(2,1)S(1)}, u32[]{:S(2)}, u32[]{:S(2)}) %collective-permute-start.84) | collective-permute-done | bytes 589856 | tf_op jit(solution)/shard_map/ppermute | solution.py:393
  384.1 3.7 collective-permute-done.81
  400.5 8.7 %collective-permute-done.78 = bf16[192,768]{1,0:T(8,128)(2,1)S(1)} collective-permute-done((bf16[192,768]{1,0:T(8,128)(2,1)}, bf16[192,768]{1,0:T(8,128)(2,1)S(1)}, u32[]{:S(2)}, u32[]{:S(2)}) %collective-permute-start.78) | collective-permute-done | bytes 294944 | tf_op jit(solution)/shard_map/ppermute | solution.py:403
  (453 shorter events, 177.5 us)
Async XLA Ops:
  34.1 17.9 %collective-permute-start.27 = (bf16[192,768]{1,0:T(8,128)(2,1)}, bf16[192,768]{1,0:T(8,128)(2,1)S(1)}, u32[]{:S(2)}, u32[]{:S(2)}) collective-permute-start(bf16[192,768]{1,0:T(8,128)(2,1)} %pad_maximum_fusion), channel_id=1, source_target_pairs={{0,3},{1,0},{2,1},{3,2},{4,7},{5,4},{6,5},{7,6},{8,11},{9,8},{10,9... | collective-permute-start | bytes 884744 | tf_op jit(solution)/shard_map/ppermute | solution.py:400
  90.0 27.0 %collective-permute-start.44 = (bf16[192,768]{1,0:T(8,128)(2,1)S(1)}, bf16[192,768]{1,0:T(8,128)(2,1)S(1)}, u32[]{:S(2)}, u32[]{:S(2)}) collective-permute-start(bf16[192,768]{1,0:T(8,128)(2,1)S(1)} %collective-permute-done.43.refs_3_), channel_id=1, source_target_pairs={{0,8},{4,20},{8,0},{12,28},{16,24},{20,4},{24,16},{28,12},{1,9},{5... | collective-permute-start | bytes 884744 | tf_op jit(solution)/shard_map/ppermute | solution.py:393
  91.2 26.7 %collective-permute-start.32 = (bf16[192,768]{1,0:T(8,128)(2,1)S(1)}, bf16[192,768]{1,0:T(8,128)(2,1)S(1)}, u32[]{:S(2)}, u32[]{:S(2)}) collective-permute-start(bf16[192,768]{1,0:T(8,128)(2,1)S(1)} %collective-permute-done.28.refs_1_), channel_id=1, source_target_pairs={{0,4},{4,0},{8,12},{12,8},{16,20},{20,16},{24,28},{28,24},{1,5},{5... | collective-permute-start | bytes 884744 | tf_op jit(solution)/shard_map/ppermute | solution.py:393
  91.2 26.8 %collective-permute-start.33 = (bf16[192,768]{1,0:T(8,128)(2,1)S(1)}, bf16[192,768]{1,0:T(8,128)(2,1)S(1)}, u32[]{:S(2)}, u32[]{:S(2)}) collective-permute-start(bf16[192,768]{1,0:T(8,128)(2,1)S(1)} %collective-permute-done.29.refs_2_), channel_id=1, source_target_pairs={{0,4},{4,0},{8,12},{12,8},{16,20},{20,16},{24,28},{28,24},{1,5},{5... | collective-permute-start | bytes 884744 | tf_op jit(solution)/shard_map/ppermute | solution.py:393
  91.7 26.7 %collective-permute-start.38 = (bf16[192,768]{1,0:T(8,128)(2,1)S(1)}, bf16[192,768]{1,0:T(8,128)(2,1)S(1)}, u32[]{:S(2)}, u32[]{:S(2)}) collective-permute-start(bf16[192,768]{1,0:T(8,128)(2,1)S(1)} %collective-permute-done.36.refs_1_), channel_id=1, source_target_pairs={{0,16},{4,12},{8,24},{12,4},{16,0},{20,28},{24,8},{28,20},{1,17},{... | collective-permute-start | bytes 884744 | tf_op jit(solution)/shard_map/ppermute | solution.py:393
  92.8 26.7 %collective-permute-start.34 = (bf16[192,768]{1,0:T(8,128)(2,1)S(1)}, bf16[192,768]{1,0:T(8,128)(2,1)S(1)}, u32[]{:S(2)}, u32[]{:S(2)}) collective-permute-start(bf16[192,768]{1,0:T(8,128)(2,1)S(1)} %collective-permute-done.30.refs_3_), channel_id=1, source_target_pairs={{0,4},{4,0},{8,12},{12,8},{16,20},{20,16},{24,28},{28,24},{1,5},{5... | collective-permute-start | bytes 884744 | tf_op jit(solution)/shard_map/ppermute | solution.py:393
  117.0 27.4 %collective-permute-start.45 = (bf16[192,768]{1,0:T(8,128)(2,1)S(1)}, bf16[192,768]{1,0:T(8,128)(2,1)S(1)}, u32[]{:S(2)}, u32[]{:S(2)}) collective-permute-start(bf16[192,768]{1,0:T(8,128)(2,1)S(1)} %collective-permute-done.43.refs_3_), channel_id=1, source_target_pairs={{0,16},{4,12},{8,24},{12,4},{16,0},{20,28},{24,8},{28,20},{1,17},{... | collective-permute-start | bytes 884744 | tf_op jit(solution)/shard_map/ppermute | solution.py:393
  117.9 27.0 %collective-permute-start.40 = (bf16[192,768]{1,0:T(8,128)(2,1)S(1)}, bf16[192,768]{1,0:T(8,128)(2,1)S(1)}, u32[]{:S(2)}, u32[]{:S(2)}) collective-permute-start(bf16[192,768]{1,0:T(8,128)(2,1)S(1)} %collective-permute-done.36.refs_1_), channel_id=1, source_target_pairs={{0,4},{4,0},{8,12},{12,8},{16,20},{20,16},{24,28},{28,24},{1,5},{5... | collective-permute-start | bytes 884744 | tf_op jit(solution)/shard_map/ppermute | solution.py:393
  118.0 26.9 %collective-permute-start.41 = (bf16[192,768]{1,0:T(8,128)(2,1)S(1)}, bf16[192,768]{1,0:T(8,128)(2,1)S(1)}, u32[]{:S(2)}, u32[]{:S(2)}) collective-permute-start(bf16[192,768]{1,0:T(8,128)(2,1)S(1)} %collective-permute-done.37.refs_2_), channel_id=1, source_target_pairs={{0,4},{4,0},{8,12},{12,8},{16,20},{20,16},{24,28},{28,24},{1,5},{5... | collective-permute-start | bytes 884744 | tf_op jit(solution)/shard_map/ppermute | solution.py:393
  118.4 27.0 %collective-permute-start.46 = (bf16[192,768]{1,0:T(8,128)(2,1)S(1)}, bf16[192,768]{1,0:T(8,128)(2,1)S(1)}, u32[]{:S(2)}, u32[]{:S(2)}) collective-permute-start(bf16[192,768]{1,0:T(8,128)(2,1)S(1)} %collective-permute-done.44.refs_4_), channel_id=1, source_target_pairs={{0,16},{4,12},{8,24},{12,4},{16,0},{20,28},{24,8},{28,20},{1,17},{... | collective-permute-start | bytes 884744 | tf_op jit(solution)/shard_map/ppermute | solution.py:393
  119.5 25.9 %collective-permute-start.42 = (bf16[192,768]{1,0:T(8,128)(2,1)S(1)}, bf16[192,768]{1,0:T(8,128)(2,1)S(1)}, u32[]{:S(2)}, u32[]{:S(2)}) collective-permute-start(bf16[192,768]{1,0:T(8,128)(2,1)S(1)} %collective-permute-done.38.refs_3_), channel_id=1, source_target_pairs={{0,4},{4,0},{8,12},{12,8},{16,20},{20,16},{24,28},{28,24},{1,5},{5... | collective-permute-start | bytes 884744 | tf_op jit(solution)/shard_map/ppermute | solution.py:393
  144.4 25.6 %collective-permute-start.47 = (bf16[192,768]{1,0:T(8,128)(2,1)S(1)}, bf16[192,768]{1,0:T(8,128)(2,1)S(1)}, u32[]{:S(2)}, u32[]{:S(2)}) collective-permute-start(bf16[192,768]{1,0:T(8,128)(2,1)S(1)} %collective-permute-done.43.refs_3_), channel_id=1, source_target_pairs={{0,4},{4,0},{8,12},{12,8},{16,20},{20,16},{24,28},{28,24},{1,5},{5... | collective-permute-start | bytes 884744 | tf_op jit(solution)/shard_map/ppermute | solution.py:393
  144.9 25.1 %collective-permute-start.48 = (bf16[192,768]{1,0:T(8,128)(2,1)S(1)}, bf16[192,768]{1,0:T(8,128)(2,1)S(1)}, u32[]{:S(2)}, u32[]{:S(2)}) collective-permute-start(bf16[192,768]{1,0:T(8,128)(2,1)S(1)} %collective-permute-done.44.refs_4_), channel_id=1, source_target_pairs={{0,4},{4,0},{8,12},{12,8},{16,20},{20,16},{24,28},{28,24},{1,5},{5... | collective-permute-start | bytes 884744 | tf_op jit(solution)/shard_map/ppermute | solution.py:393
  144.9 25.1 %collective-permute-start.49 = (bf16[192,768]{1,0:T(8,128)(2,1)S(1)}, bf16[192,768]{1,0:T(8,128)(2,1)S(1)}, u32[]{:S(2)}, u32[]{:S(2)}) collective-permute-start(bf16[192,768]{1,0:T(8,128)(2,1)S(1)} %collective-permute-done.45.refs_5_), channel_id=1, source_target_pairs={{0,4},{4,0},{8,12},{12,8},{16,20},{20,16},{24,28},{28,24},{1,5},{5... | collective-permute-start | bytes 884744 | tf_op jit(solution)/shard_map/ppermute | solution.py:393
  145.4 24.6 %collective-permute-start.50 = (bf16[192,768]{1,0:T(8,128)(2,1)S(1)}, bf16[192,768]{1,0:T(8,128)(2,1)S(1)}, u32[]{:S(2)}, u32[]{:S(2)}) collective-permute-start(bf16[192,768]{1,0:T(8,128)(2,1)S(1)} %collective-permute-done.46.refs_6_), channel_id=1, source_target_pairs={{0,4},{4,0},{8,12},{12,8},{16,20},{20,16},{24,28},{28,24},{1,5},{5... | collective-permute-start | bytes 884744 | tf_op jit(solution)/shard_map/ppermute | solution.py:393
  293.2 51.1 %collective-permute-start.75 = (bf16[4,192,768]{2,1,0:T(8,128)(2,1)}, bf16[4,192,768]{2,1,0:T(8,128)(2,1)}, u32[]{:S(2)}, u32[]{:S(2)}) collective-permute-start(bf16[4,192,768]{2,1,0:T(8,128)(2,1)} %copy-done.29), channel_id=1, source_target_pairs={{0,4},{4,0},{8,12},{12,8},{16,20},{20,16},{24,28},{28,24},{1,5},{5... | collective-permute-start | bytes 3538952 | tf_op jit(solution)/shard_map/ppermute | solution.py:393
  293.7 52.3 %collective-permute-start.79 = (bf16[4,192,768]{2,1,0:T(8,128)(2,1)}, bf16[4,192,768]{2,1,0:T(8,128)(2,1)}, u32[]{:S(2)}, u32[]{:S(2)}) collective-permute-start(bf16[4,192,768]{2,1,0:T(8,128)(2,1)} %copy-done.32), channel_id=1, source_target_pairs={{0,4},{4,0},{8,12},{12,8},{16,20},{20,16},{24,28},{28,24},{1,5},{5... | collective-permute-start | bytes 3538952 | tf_op jit(solution)/shard_map/ppermute | solution.py:393
  308.2 43.5 %collective-permute-start.83 = (bf16[4,192,768]{2,1,0:T(8,128)(2,1)S(1)}, bf16[4,192,768]{2,1,0:T(8,128)(2,1)S(1)}, u32[]{:S(2)}, u32[]{:S(2)}) collective-permute-start(bf16[4,192,768]{2,1,0:T(8,128)(2,1)S(1)} %copy-done.31), channel_id=1, source_target_pairs={{0,4},{4,0},{8,12},{12,8},{16,20},{20,16},{24,28},{28,24},{1,5},{5... | collective-permute-start | bytes 3538952 | tf_op jit(solution)/shard_map/ppermute | solution.py:393
  323.4 26.6 %collective-permute-start.73 = (bf16[2,192,768]{2,1,0:T(8,128)(2,1)S(1)}, bf16[2,192,768]{2,1,0:T(8,128)(2,1)S(1)}, u32[]{:S(2)}, u32[]{:S(2)}) collective-permute-start(bf16[2,192,768]{2,1,0:T(8,128)(2,1)S(1)} %slice.361), channel_id=1, source_target_pairs={{0,8},{4,20},{8,0},{12,28},{16,24},{20,4},{24,16},{28,12},{1,9},{5... | collective-permute-start | bytes 1769480 | tf_op jit(solution)/shard_map/ppermute | solution.py:393
  343.5 49.3 %collective-permute-start.59 = (bf16[96,768]{1,0:T(8,128)(2,1)S(1)}, bf16[96,768]{1,0:T(8,128)(2,1)S(1)}, u32[]{:S(2)}, u32[]{:S(2)}) collective-permute-start(bf16[96,768]{1,0:T(8,128)(2,1)S(1)} %fusion.24), channel_id=1, source_target_pairs={{0,16},{4,12},{8,24},{12,4},{16,0},{20,28},{24,8},{28,20},{1,17},{... | collective-permute-start | bytes 442376 | tf_op jit(solution)/shard_map/ppermute | solution.py:393
  344.3 49.7 %collective-permute-start.63 = (bf16[96,768]{1,0:T(8,128)(2,1)S(1)}, bf16[96,768]{1,0:T(8,128)(2,1)S(1)}, u32[]{:S(2)}, u32[]{:S(2)}) collective-permute-start(bf16[96,768]{1,0:T(8,128)(2,1)S(1)} %fusion.19), channel_id=1, source_target_pairs={{0,1},{1,2},{2,3},{3,0},{4,5},{5,6},{6,7},{7,4},{8,9},{9,10},{10,1... | collective-permute-start | bytes 442376 | tf_op jit(solution)/shard_map/ppermute | solution.py:403
  346.0 51.1 %collective-permute-start.67 = (bf16[96,768]{1,0:T(8,128)(2,1)S(1)}, bf16[96,768]{1,0:T(8,128)(2,1)S(1)}, u32[]{:S(2)}, u32[]{:S(2)}) collective-permute-start(bf16[96,768]{1,0:T(8,128)(2,1)S(1)} %fusion.17), channel_id=1, source_target_pairs={{0,2},{1,3},{2,0},{3,1},{4,6},{5,7},{6,4},{7,5},{8,10},{9,11},{10,... | collective-permute-start | bytes 442376 | tf_op jit(solution)/shard_map/ppermute | solution.py:403
  359.9 21.1 %collective-permute-start.84 = (bf16[2,192,768]{2,1,0:T(8,128)(2,1)S(1)}, bf16[2,192,768]{2,1,0:T(8,128)(2,1)S(1)}, u32[]{:S(2)}, u32[]{:S(2)}) collective-permute-start(bf16[2,192,768]{2,1,0:T(8,128)(2,1)S(1)} %slice.358), channel_id=1, source_target_pairs={{0,8},{4,20},{8,0},{12,28},{16,24},{20,4},{24,16},{28,12},{1,9},{5... | collective-permute-start | bytes 1769480 | tf_op jit(solution)/shard_map/ppermute | solution.py:393
  394.0 18.3 %collective-permute-start.82 = (bf16[192,768]{1,0:T(8,128)(2,1)}, bf16[192,768]{1,0:T(8,128)(2,1)S(1)}, u32[]{:S(2)}, u32[]{:S(2)}) collective-permute-start(bf16[192,768]{1,0:T(8,128)(2,1)} %fusion.3), channel_id=1, source_target_pairs={{0,2},{1,3},{2,0},{3,1},{4,6},{5,7},{6,4},{7,5},{8,10},{9,11},{10,... | collective-permute-start | bytes 884744 | tf_op jit(solution)/shard_map/ppermute | solution.py:403
  (155 other events, 1485.8 us)
